TPU v7x, 32 devices: a whole 2x2x4 slice. The times are simulated.
32 devices in a mesh: groups: 1, tile: 32 (over z, y, x, core).
Axes of the slice: x: 2, y: 2, z: 4, core: 2. Of those that a mesh axis runs over, the one named last changes fastest.
Arguments:
- fields: bfloat16 [96, 512, 1024], P('groups', 'tile'), may hold values from -6 to 6
- kernel: float32 [9, 1024], replicated, may hold values from -2 to 2
- norm_gain: float32 [1024], replicated, may hold values from 0.5 to 2
- land_bias: float32 [1024], replicated, may hold values from -6 to 6
- w_in: bfloat16 [1024, 1024], replicated, may hold values from -0.1875 to 0.1875
- w_out: bfloat16 [1024, 1024], replicated, may hold values from -0.1875 to 0.1875
- land_mask: int32 [96, 512], P('groups', 'tile'), may hold values 0 or 1
- cotangent: bfloat16 [96, 512, 1024], P('groups', 'tile'), may hold values from -6 to 6
Outputs:
- grad_fields: bfloat16 [96, 512, 1024], P('groups', 'tile')
- grad_w_in: float32 [1024, 1024], P('groups')
- grad_w_out: float32 [1024, 1024], P('groups')
- grad_kernel: float32 [9, 1024], P('groups')
- grad_gain: float32 [1024], P('groups')
- grad_land: float32 [1024], P('groups')
All inputs are finite; a program needn't handle non-finite values. No bound on the sum of `land_mask` on one device may be relied on, other than what follows from the above.
Results may differ from a plain program's by a relative error of at most 0.0075.
Values may be sent and summed in bfloat16 or wider, within the bound.
A program may use at most 128 MiB of HBM per device.

v0:
```python
import jax
import jax.numpy as jnp
from jax import lax
from jax.sharding import PartitionSpec as P

EPS = 1e-06
INV_ROOT_TWO = 0.7071067811865476
INV_ROOT_TWO_PI = 0.3989422804014327


def extended(cells, sides, width):
    for axis, dim in sides:
        count = lax.axis_size(axis)
        head = lax.slice_in_dim(cells, 0, width, axis=dim)
        tail = lax.slice_in_dim(cells, cells.shape[dim] - width, cells.shape[dim], axis=dim)
        cells = jnp.concatenate(
            [
                lax.ppermute(tail, axis, [(i, (i + 1) % count) for i in range(count)]),
                cells,
                lax.ppermute(head, axis, [((i + 1) % count, i) for i in range(count)]),
            ],
            axis=dim,
        )
    return cells


def swapped(block, axis, distance):
    count = lax.axis_size(axis)
    route = []
    for low in range(count):
        high = low | 1 << distance
        if high != low and high < count:
            route += [(low, high), (high, low)]
    return lax.ppermute(block, axis, route)


def extend(field):
    widened = extended(field, (("tile", 1),), 1)
    polar = jnp.stack([widened[0], widened[-1]])
    partner = swapped(polar, "tile", lax.axis_size("tile").bit_length() - 2)
    return (widened, partner)


def body(fields, kernel, norm_gain, land_bias, w_in, w_out, land_mask, cotangent):
    rows, cols, chans = fields.shape
    widened, partner = extend(fields)
    padded = jnp.concatenate([partner[:1], widened, partner[1:]], axis=0)
    land = land_mask.astype(jnp.float32)[:, :, None]
    depth = jnp.zeros((rows, cols, chans), jnp.float32)
    for row in range(3):
        for col in range(3):
            depth = depth + kernel[3 * row + col] * padded[
                row : row + rows, col : col + cols
            ].astype(jnp.float32)
    depth = depth + land * land_bias
    scale = lax.rsqrt(jnp.mean(depth * depth, axis=-1, keepdims=True) + EPS)
    normed = (depth * scale * norm_gain).astype(jnp.bfloat16).reshape(-1, chans)
    pre = jnp.dot(normed, w_in, preferred_element_type=jnp.float32)
    cdf = 0.5 * (1.0 + lax.erf(pre * INV_ROOT_TWO))
    hidden = (pre * cdf).astype(jnp.bfloat16)
    upstream = cotangent.reshape(-1, chans)
    grad_w_out = jnp.dot(hidden.T, upstream, preferred_element_type=jnp.float32)
    g_hidden = jnp.dot(upstream, w_out.T, preferred_element_type=jnp.float32)
    slope = cdf + pre * jnp.exp(-0.5 * pre * pre) * INV_ROOT_TWO_PI
    g_pre = (g_hidden * slope).astype(jnp.bfloat16)
    grad_w_in = jnp.dot(normed.T, g_pre, preferred_element_type=jnp.float32)
    g_normed = jnp.dot(g_pre, w_in.T, preferred_element_type=jnp.float32).reshape(rows, cols, chans)
    grad_gain = jnp.sum(g_normed * depth * scale, axis=(0, 1))
    weighted = g_normed * norm_gain
    inner = jnp.mean(weighted * depth, axis=-1, keepdims=True)
    g_depth = (scale * weighted - depth * scale * scale * scale * inner).astype(jnp.bfloat16)
    g_float = g_depth.astype(jnp.float32)
    tap_terms = []
    for row in range(3):
        for col in range(3):
            window = padded[row : row + rows, col : col + cols].astype(jnp.float32)
            tap_terms.append(jnp.sum(g_float * window, axis=(0, 1)))
    grad_kernel = jnp.stack(tap_terms)
    grad_land = jnp.sum(g_float * land, axis=(0, 1))
    g_wide, g_partner = extend(g_depth)
    empty_row = jnp.zeros((1, cols + 2, chans), jnp.bfloat16)
    g_padded = jnp.concatenate([empty_row, g_wide, empty_row], axis=0)
    g_conv = jnp.zeros((rows, cols, chans), jnp.float32)
    north = jnp.zeros((cols, chans), jnp.float32)
    south = jnp.zeros((cols, chans), jnp.float32)
    for row in range(3):
        for col in range(3):
            tap = kernel[3 * row + col]
            g_conv = g_conv + tap * g_padded[
                2 - row : 2 - row + rows, 2 - col : 2 - col + cols
            ].astype(jnp.float32)
    for col in range(3):
        north = north + kernel[col] * g_partner[0, 2 - col : 2 - col + cols].astype(jnp.float32)
        south = south + kernel[6 + col] * g_partner[1, 2 - col : 2 - col + cols].astype(jnp.float32)
    g_conv = g_conv.at[0].add(north)
    g_conv = g_conv.at[rows - 1].add(south)
    grad_fields = (g_conv + cotangent.astype(jnp.float32)).astype(jnp.bfloat16)
    grad_w_in, grad_w_out, grad_kernel, grad_gain, grad_land = lax.psum(
        (grad_w_in, grad_w_out, grad_kernel, grad_gain, grad_land), "tile"
    )
    return (grad_fields, grad_w_in, grad_w_out, grad_kernel, grad_gain, grad_land)


def solution(mesh):
    placed = (
        P("groups", "tile", None),
        P(),
        P(),
        P(),
        P(),
        P(),
        P("groups", "tile"),
        P("groups", "tile", None),
    )
    return jax.shard_map(
        body,
        mesh=mesh,
        in_specs=placed,
        out_specs=(
            P("groups", "tile", None),
            P("groups", None),
            P("groups", None),
            P("groups", None),
            P("groups"),
            P("groups"),
        ),
        check_vma=False,
    )
```

profile of v0, /device:TPU:0, one launch (start us, length us, event | category | flops | bytes accessed | tf_op | source)
XLA Modules:
  0.0 279.3 jit_solution(5360662369699728390)
XLA Ops:
  7.3 2.7 fusion.47
  10.1 6.4 %collective-permute-start.1 = (bf16[96,1,1024]{2,0,1:T(8,128)(2,1)S(1)}, bf16[96,1,1024]{2,0,1:T(8,128)(2,1)S(1)}, u32[]{:S(2)}, u32[]{:S(2)}) collective-permute-start(bf16[96,1,1024]{2,0,1:T(8,128)(2,1)S(1)} %copy.39), channel_id=1, source_target_pairs={{1,0},{2,1},{3,2},{4,3},{5,4},{6,5},{7,6},{8,7},{9,8},{10,9},{11,1... | collective-permute-start | bytes 589832 | tf_op jit(solution)/shard_map/ppermute | solution.py:20
  16.6 3.1 %collective-permute-done.1 = bf16[96,1,1024]{2,0,1:T(8,128)(2,1)S(1)} collective-permute-done((bf16[96,1,1024]{2,0,1:T(8,128)(2,1)S(1)}, bf16[96,1,1024]{2,0,1:T(8,128)(2,1)S(1)}, u32[]{:S(2)}, u32[]{:S(2)}) %collective-permute-start.1) | collective-permute-done | bytes 196640 | tf_op jit(solution)/shard_map/ppermute | solution.py:20
  19.7 0.3 copy.28
  20.0 5.3 %collective-permute-done = bf16[96,1,1024]{2,0,1:T(8,128)(2,1)S(1)} collective-permute-done((bf16[96,1,1024]{2,0,1:T(8,128)(2,1)S(1)}, bf16[96,1,1024]{2,0,1:T(8,128)(2,1)S(1)}, u32[]{:S(2)}, u32[]{:S(2)}) %collective-permute-start) | collective-permute-done | bytes 196640 | tf_op jit(solution)/shard_map/ppermute | solution.py:18
  25.3 0.3 copy.27
  25.6 0.9 fusion.39
  26.8 5.3 %collective-permute-done.2 = bf16[2,18,1024]{2,1,0:T(8,128)(2,1)S(1)} collective-permute-done((bf16[2,18,1024]{2,1,0:T(8,128)(2,1)S(1)}, bf16[2,18,1024]{2,1,0:T(8,128)(2,1)S(1)}, u32[]{:S(2)}, u32[]{:S(2)}) %collective-permute-start.2) | collective-permute-done | bytes 73760 | tf_op jit(solution)/shard_map/ppermute | solution.py:34
  32.1 11.0 %maximum_maximum_fusion = (bf16[97,18,1024]{2,1,0:T(8,128)(2,1)S(1)}, bf16[97,18,1024]{2,1,0:T(8,128)(2,1)S(1)}) fusion(bf16[96,1,1024]{2,1,0:T(2,128)(2,1)S(1)} %copy.28, bf16[96,16,1024]{2,1,0:T(8,128)(2,1)} %param.12, bf16[96,1,1024]{2,1,0:T(2,128)(2,1)S(1)} %copy.27, bf16[1,18,1024]{2,1,0:T(8,128)(2,1)S(1)} %get-tuple-element.71, ...), kind=kLoop, calls=%fused_computation.59 | loop fusion | flops 28606464 | bytes 10764288 | tf_op jit(solution)/shard_map/concatenate | solution.py:47
  43.2 10.3 %multiply_reduce_fusion.2 = (f32[96,16]{1,0:T(8,128)S(1)}, f32[96,16,1024]{2,1,0:T(8,128)S(1)}) fusion(f32[1024]{0:T(1024)S(1)} %copy-done.15, f32[96,16]{1,0:T(8,128)S(1)} %copy.31, bf16[97,18,1024]{2,1,0:T(8,128)(2,1)S(1)} %get-tuple-element.66, f32[1024]{0:T(1024)S(1)} %bitcast.39, f32[1024]{0:T(1024)S(1)} %bitcast.42, f32[1024]{0:T(1024)S(1)} %bitcast.36, ...), kind=kLoop, calls=%fused_computation.58 | loop fusion | flops 56621568 | bytes 28758016 | tf_op jit(solution)/shard_map/reduce_sum | solution.py:56
  53.6 0.6 multiply_convert_fusion.1
  54.2 3.5 %fusion.50 = f32[1536,1024]{1,0:T(8,128)S(1)} fusion(bf16[1536,1024]{1,0:T(8,128)(2,1)S(1)} %bitcast.34, bf16[1024,1024]{1,0:T(8,128)(2,1)S(1)} %copy-done), kind=kOutput, calls=%fused_computation.98 | convolution fusion | flops 3221225472 | bytes 11534336 | tf_op jit(solution)/shard_map/dot_general | solution.py:58
  57.7 5.3 %fusion.30 = f32[1024,1024]{1,0:T(8,128)} fusion(bf16[1536,1024]{1,0:T(8,128)(2,1)S(1)} %bitcast.32, f32[1536,1024]{1,0:T(8,128)S(1)} %fusion.50), kind=kOutput, calls=%fused_computation.68 | convolution fusion | flops 3229089792 | bytes 13631488 | tf_op jit(solution)/shard_map/dot_general | solution.py:62
  63.1 5.5 %fusion.14 = bf16[1536,1024]{1,0:T(8,128)(2,1)S(1)} fusion(f32[1536,1024]{1,0:T(8,128)S(1)} %fusion.50, bf16[1536,1024]{1,0:T(8,128)(2,1)S(1)} %bitcast.33, bf16[1024,1024]{1,0:T(8,128)(2,1)S(1)} %copy-done.16), kind=kOutput, calls=%fused_computation.35 | convolution fusion | flops 3236954112 | bytes 14680064 | tf_op jit(solution)/shard_map/dot_general | solution.py:63
  68.6 1.7 copy-done.17
  70.3 5.0 %fusion.52 = f32[1024,1024]{1,0:T(8,128)} fusion(bf16[1536,1024]{1,0:T(8,128)(2,1)S(1)} %bitcast.35, bf16[1536,1024]{1,0:T(8,128)(2,1)S(1)} %fusion.14), kind=kOutput, calls=%fused_computation.100 | convolution fusion | flops 3221225472 | bytes 10485760 | tf_op jit(solution)/shard_map/dot_general | solution.py:66
  75.3 5.4 %fusion.51 = f32[1536,1024]{1,0:T(8,128)S(1)} fusion(bf16[1536,1024]{1,0:T(8,128)(2,1)} %copy-done.17, bf16[1024,1024]{1,0:T(8,128)(2,1)S(1)} %copy-done), kind=kOutput, calls=%fused_computation.99 | convolution fusion | flops 3221225472 | bytes 11534336 | tf_op jit(solution)/shard_map/dot_general | solution.py:67
  80.6 6.2 %multiply_reduce_fusion = (f32[1024]{0:T(1024)S(1)}, f32[96,16]{1,0:T(8,128)S(1)}) fusion(f32[96,16,1024]{2,1,0:T(8,128)S(1)} %bitcast.30, f32[96,16,1024]{2,1,0:T(8,128)} %copy-done.4, f32[96,16]{1,0:T(8,128)S(1)} %add_rsqrt_fusion, f32[1024]{0:T(1024)S(1)} %copy-done.12), kind=kLoop, calls=%fused_computation.51 | loop fusion | flops 9434624 | bytes 12603392 | tf_op jit(solution)/shard_map/reduce_sum | solution.py:68
  86.9 24.3 %fusion.28 = (f32[1024]{0:T(1024)S(1)}, f32[1024]{0:T(1024)S(1)}, f32[1024]{0:T(1024)S(1)}, f32[1024]{0:T(1024)S(1)}, f32[1024]{0:T(1024)S(1)}, /*index=5*/f32[1...) fusion(bf16[97,18,1024]{2,1,0:T(8,128)(2,1)} %copy-done.3, ...), kind=kLoop, calls=%fused_computation.49 | loop fusion | flops 69195776 | bytes 38205440 | tf_op jit(solution)/shard_map/reduce_sum | solution.py:77
  111.3 1.7 copy-done.6
  112.9 0.7 fusion.46
  113.7 0.7 collective-permute-start.4
  114.6 40.1 %all-reduce.2 = (f32[9,1024]{1,0:T(8,128)}, f32[1024]{0:T(1024)}, f32[1024]{0:T(1024)}) all-reduce(f32[9,1024]{1,0:T(8,128)S(1)} %stack.47, f32[1024]{0:T(1024)S(1)} %get-tuple-element.36, f32[1024]{0:T(1024)S(1)} %get-tuple-element.48), channel_id=1, replica_groups=mesh['groups'=1,'tile'=32] {'tile'}, use_global_device_ids=true, to_apply=%region_13.0 | all-reduce | flops 11264 | bytes 90112 | tf_op jit(solution)/shard_map/psum | solution.py:98
  154.7 0.3 copy.35
  155.0 0.3 copy.34
  155.3 4.9 %pad_maximum_fusion.1 = bf16[96,18,1024]{2,1,0:T(8,128)(2,1)S(1)} fusion(bf16[96,1,1024]{2,1,0:T(2,128)(2,1)S(1)} %copy.35, bf16[96,16,1024]{2,1,0:T(8,128)(2,1)} %copy-done.6, bf16[96,1,1024]{2,1,0:T(2,128)(2,1)S(1)} %copy.34), kind=kLoop, calls=%fused_computation.61 | loop fusion | flops 10616832 | bytes 7077888 | tf_op jit(solution)/shard_map/concatenate | solution.py:16
  160.3 2.6 collective-permute-start.5
  162.9 9.3 %fusion.19 = f32[96,16,1024]{2,1,0:T(8,128)S(1)} fusion(bf16[96,16,1024]{2,1,0:T(8,128)(2,1)S(1)} %copy-done.7, bf16[96,18,1024]{2,1,0:T(8,128)(2,1)S(1)} %pad_maximum_fusion.1, bf16[96,1,1024]{2,1,0:T(2,128)(2,1)S(1)} %copy.34, bf16[96,1,1024]{2,1,0:T(2,128)(2,1)S(1)} %copy.35, f32[1024]{0:T(1024)S(1)} %bitcast.40, f32[1024]{0:T(1024)S(1)} %bitcast.43, ...), kind=kLoop, calls=%fused_computation.40 | loop fusion | flops 50331648 | bytes 13406208 | tf_op jit(solution)/shard_map/add | solution.py:89
  172.3 3.0 %add_convert_fusion = bf16[96,16,1024]{2,1,0:T(8,128)(2,1)} fusion(f32[96,16,1024]{2,1,0:T(8,128)S(1)} %fusion.42, bf16[96,16,1024]{2,1,0:T(8,128)(2,1)S(1)} %copy-done.10), kind=kLoop, calls=%fused_computation.53 | loop fusion | flops 4718592 | bytes 12582912 | tf_op jit(solution)/shard_map/convert_element_type | solution.py:97
  175.3 90.2 %all-reduce.6.cloned.1.call-done = (f32[1024,1024]{1,0:T(8,128)}, f32[1024,1024]{1,0:T(8,128)}) async-done(((f32[1024,1024]{1,0:T(8,128)}, f32[1024,1024]{1,0:T(8,128)}), (f32[1024,1024]{1,0:T(8,128)}, f32[1024,1024]{1,0:T(8,128)})) %all-reduce.6.cloned.1.call-update) | async-done | bytes 8388624 | tf_op jit(solution)/shard_map/psum | solution.py:98
  265.5 4.9 %copy.44 = f32[1024,1024]{1,0:T(8,128)} copy(f32[1024,1024]{1,0:T(8,128)} %get-tuple-element.83) | data formatting | bytes 8388608
  270.4 2.0 copy.45
  (57 shorter events, 0.9 us)
Async XLA Ops:
  7.2 47.0 %copy-start = (bf16[1024,1024]{1,0:T(8,128)(2,1)S(1)}, bf16[1024,1024]{1,0:T(8,128)(2,1)}, u32[]{:S(2)}) copy-start(bf16[1024,1024]{1,0:T(8,128)(2,1)} %param.16) | copy-start | bytes 6291460
  7.2 19.4 %copy-start.13 = (f32[9,1024]{1,0:T(8,128)S(1)}, f32[9,1024]{1,0:T(8,128)}, u32[]{:S(2)}) copy-start(f32[9,1024]{1,0:T(8,128)} %param.13) | copy-start | bytes 110596
  7.2 19.5 %copy-start.14 = (s32[96,16]{0,1:T(8,128)S(1)}, s32[96,16]{0,1:T(8,128)}, u32[]{:S(2)}) copy-start(s32[96,16]{0,1:T(8,128)} %param.18) | copy-start | bytes 18436
  7.2 258.3 %all-reduce.6.cloned.1.call-start = ((), (), s32[]{:S(2)}) async-start(), calls=%async_computation | async-start | bytes 16777216 | tf_op jit(solution)/shard_map/psum | solution.py:98
  10.1 9.6 %collective-permute-start.1 = (bf16[96,1,1024]{2,0,1:T(8,128)(2,1)S(1)}, bf16[96,1,1024]{2,0,1:T(8,128)(2,1)S(1)}, u32[]{:S(2)}, u32[]{:S(2)}) collective-permute-start(bf16[96,1,1024]{2,0,1:T(8,128)(2,1)S(1)} %copy.39), channel_id=1, source_target_pairs={{1,0},{2,1},{3,2},{4,3},{5,4},{6,5},{7,6},{8,7},{9,8},{10,9},{11,1... | collective-permute-start | bytes 589832 | tf_op jit(solution)/shard_map/ppermute | solution.py:20
  16.6 8.7 %collective-permute-start = (bf16[96,1,1024]{2,0,1:T(8,128)(2,1)S(1)}, bf16[96,1,1024]{2,0,1:T(8,128)(2,1)S(1)}, u32[]{:S(2)}, u32[]{:S(2)}) collective-permute-start(bf16[96,1,1024]{2,0,1:T(8,128)(2,1)S(1)} %copy.38), channel_id=1, source_target_pairs={{0,1},{1,2},{2,3},{3,4},{4,5},{5,6},{6,7},{7,8},{8,9},{9,10},{10,1... | collective-permute-start | bytes 589832 | tf_op jit(solution)/shard_map/ppermute | solution.py:18
  26.5 5.6 %collective-permute-start.2 = (bf16[2,18,1024]{2,1,0:T(8,128)(2,1)S(1)}, bf16[2,18,1024]{2,1,0:T(8,128)(2,1)S(1)}, u32[]{:S(2)}, u32[]{:S(2)}) collective-permute-start(bf16[2,18,1024]{2,1,0:T(8,128)(2,1)S(1)} %fusion.39), channel_id=1, source_target_pairs={{0,16},{16,0},{1,17},{17,1},{2,18},{18,2},{3,19},{19,3},{4,20},{20... | collective-permute-start | bytes 221192 | tf_op jit(solution)/shard_map/ppermute | solution.py:34
  32.1 11.1 %copy-start.5 = (bf16[96,16,1024]{2,1,0:T(8,128)(2,1)S(1)}, bf16[96,16,1024]{2,1,0:T(8,128)(2,1)}, u32[]{:S(2)}) copy-start(bf16[96,16,1024]{2,1,0:T(8,128)(2,1)} %param.12) | copy-start | bytes 9437188
  32.1 11.1 %copy-start.15 = (f32[1024]{0:T(1024)S(1)}, f32[1024]{0:T(1024)}, u32[]{:S(2)}) copy-start(f32[1024]{0:T(1024)} %param.15) | copy-start | bytes 12292
  43.2 10.4 %copy-start.2 = (bf16[97,18,1024]{2,1,0:T(8,128)(2,1)}, bf16[97,18,1024]{2,1,0:T(8,128)(2,1)S(1)}, u32[]{:S(2)}) copy-start(bf16[97,18,1024]{2,1,0:T(8,128)(2,1)S(1)} %get-tuple-element.65) | copy-start | bytes 10727428
  43.2 10.4 %copy-start.3 = (bf16[97,18,1024]{2,1,0:T(8,128)(2,1)}, bf16[97,18,1024]{2,1,0:T(8,128)(2,1)S(1)}, u32[]{:S(2)}) copy-start(bf16[97,18,1024]{2,1,0:T(8,128)(2,1)S(1)} %get-tuple-element.66) | copy-start | bytes 10727428
  43.2 10.4 %copy-start.12 = (f32[1024]{0:T(1024)S(1)}, f32[1024]{0:T(1024)}, u32[]{:S(2)}) copy-start(f32[1024]{0:T(1024)} %param.14) | copy-start | bytes 12292
  53.6 4.2 %copy-start.4 = (f32[96,16,1024]{2,1,0:T(8,128)}, f32[96,16,1024]{2,1,0:T(8,128)S(1)}, u32[]{:S(2)}) copy-start(f32[96,16,1024]{2,1,0:T(8,128)S(1)} %get-tuple-element.62) | copy-start | bytes 18874372
  54.2 3.5 %copy-start.9 = (bf16[96,16,1024]{2,1,0:T(8,128)(2,1)S(1)}, bf16[96,16,1024]{2,1,0:T(8,128)(2,1)}, u32[]{:S(2)}) copy-start(bf16[96,16,1024]{2,1,0:T(8,128)(2,1)} %param.19) | copy-start | bytes 9437188
  57.7 5.4 %copy-start.16 = (bf16[1024,1024]{1,0:T(8,128)(2,1)S(1)}, bf16[1024,1024]{1,0:T(8,128)(2,1)}, u32[]{:S(2)}) copy-start(bf16[1024,1024]{1,0:T(8,128)(2,1)} %param.17) | copy-start | bytes 6291460
  68.6 1.7 copy-start.17
  80.6 6.2 %copy-start.8 = (f32[1536,1024]{1,0:T(8,128)}, f32[1536,1024]{1,0:T(8,128)S(1)}, u32[]{:S(2)}) copy-start(f32[1536,1024]{1,0:T(8,128)S(1)} %fusion.51) | copy-start | bytes 18874372
  111.3 1.7 copy-start.6
  113.7 41.0 %collective-permute-start.4 = (bf16[96,1,1024]{2,0,1:T(8,128)(2,1)S(1)}, bf16[96,1,1024]{2,0,1:T(8,128)(2,1)S(1)}, u32[]{:S(2)}, u32[]{:S(2)}) collective-permute-start(bf16[96,1,1024]{2,0,1:T(8,128)(2,1)S(1)} %copy.33), channel_id=1, source_target_pairs={{1,0},{2,1},{3,2},{4,3},{5,4},{6,5},{7,6},{8,7},{9,8},{10,9},{11,1... | collective-permute-start | bytes 589832 | tf_op jit(solution)/shard_map/ppermute | solution.py:20
  114.5 40.6 %collective-permute-start.3 = (bf16[96,1,1024]{2,0,1:T(8,128)(2,1)S(1)}, bf16[96,1,1024]{2,0,1:T(8,128)(2,1)S(1)}, u32[]{:S(2)}, u32[]{:S(2)}) collective-permute-start(bf16[96,1,1024]{2,0,1:T(8,128)(2,1)S(1)} %copy.32), channel_id=1, source_target_pairs={{0,1},{1,2},{2,3},{3,4},{4,5},{5,6},{6,7},{7,8},{8,9},{9,10},{10,1... | collective-permute-start | bytes 589832 | tf_op jit(solution)/shard_map/ppermute | solution.py:18
  154.7 8.2 %copy-start.7 = (bf16[96,16,1024]{2,1,0:T(8,128)(2,1)S(1)}, bf16[96,16,1024]{2,1,0:T(8,128)(2,1)}, u32[]{:S(2)}) copy-start(bf16[96,16,1024]{2,1,0:T(8,128)(2,1)} %copy-done.6) | copy-start | bytes 9437188
  160.3 12.0 %copy-start.10 = (bf16[96,16,1024]{2,1,0:T(8,128)(2,1)S(1)}, bf16[96,16,1024]{2,1,0:T(8,128)(2,1)}, u32[]{:S(2)}) copy-start(bf16[96,16,1024]{2,1,0:T(8,128)(2,1)} %param.19) | copy-start | bytes 9437188
  160.3 11.9 %collective-permute-start.5 = (bf16[2,18,1024]{2,1,0:T(8,128)(2,1)S(1)}, bf16[2,18,1024]{2,1,0:T(8,128)(2,1)S(1)}, u32[]{:S(2)}, u32[]{:S(2)}) collective-permute-start(bf16[2,18,1024]{2,1,0:T(8,128)(2,1)S(1)} %pad_maximum_fusion.6), channel_id=1, source_target_pairs={{0,16},{16,0},{1,17},{17,1},{2,18},{18,2},{3,19},{19,3},{4,20},{20... | collective-permute-start | bytes 221192 | tf_op jit(solution)/shard_map/ppermute | solution.py:34
  265.5 4.9 %copy-start.11 = (f32[1024,1024]{1,0:T(8,128)S(1)}, f32[1024,1024]{1,0:T(8,128)}, u32[]{:S(2)}) copy-start(f32[1024,1024]{1,0:T(8,128)} %get-tuple-element.84) | copy-start | bytes 12582916
  265.5 7.0 %copy-start.1 = (bf16[1024,1024]{1,0:T(8,128)(2,1)S(1)}, bf16[1024,1024]{1,0:T(8,128)(2,1)}, u32[]{:S(2)}) copy-start(bf16[1024,1024]{1,0:T(8,128)(2,1)} %param.16) | copy-start | bytes 6291460
Sparse Core Ops, SparseCore 0:
  87.0 178.4 all-reduce.5
where the time goes:
time: 280 us; the launch traced here: 279 us
  waiting for transfers between devices  104 us (37%)
  other arithmetic  70.7 us (25%)
  blocking collectives  40.1 us (14%)
  matrix products  24.7 us (9%)
  local copies, waits for them, and re-layouts  15.5 us (6%)
  between operations  14.5 us (5%)
  starting transfers between devices  9.95 us (4%)
    psum x1, waiting for transfers between devices, body(): lax.psum((grad_w_in, grad_w_out, grad_kernel, grad_gain, grad_land), 'tile')  90.2 us
    psum x1, blocking collectives, body(): lax.psum((grad_w_in, grad_w_out, grad_kernel, grad_gain, grad_land), 'tile')  40.1 us
    reduce_sum x1, other arithmetic, body(): tap_terms.append(jnp.sum(g_float * window, axis=(0, 1)))  24.3 us
    concatenate x1, other arithmetic, body(): padded = jnp.concatenate([partner[:1], widened, partner[1:]], axis=0)  11 us
    unnamed x40, local copies, waits for them, and re-layouts  10.5 us
    reduce_sum x1, other arithmetic, body(): scale = lax.rsqrt(jnp.mean(depth * depth, axis=-1, keepdims=True) + EPS)  10.3 us
    add x1, other arithmetic, body(): g_conv + tap * g_padded[2 - row:2 - row + rows, 2 - col:2 - col + cols].a...  9.28 us
    ppermute x2, starting transfers between devices, extended(): lax.ppermute(head, axis, [((i + 1) % count, i) for i in range(count)])  7.12 us
  transfers between devices with their start and end apart: 7, of which 4 were waited for; matrix products, arithmetic and copies ran while one was open for 16% of the time, Pallas kernels for 0%

commit v1 on v0

v1 whole, which is shorter than its diff:
```python
import functools

import jax
import jax.numpy as jnp
from jax import lax
from jax.experimental import pallas as pl
from jax.experimental.pallas import tpu as pltpu
from jax.sharding import PartitionSpec as P

EPS = 1e-06
INV_ROOT_TWO = 0.7071067811865476
INV_ROOT_TWO_PI = 0.3989422804014327
F32 = jnp.float32
BF16 = jnp.bfloat16
LANES = 256
NT = (((1,), (1,)), ((), ()))
TN = (((0,), (0,)), ((), ()))


def block_kernel(
    count, fields_hbm, cot_hbm, w_in_hbm, w_out_hbm, taps, gain, bias, land,
    out_hbm, gw_hbm, small_out,
    F, COT, WI, WO, D, NRM, GH, HID, GP, GX, PRE, SC, G, RB, RP, A,
    COL, HX, EDGE, CS, CR, KS, KR, GA, LA, SS, SR,
    load_sem, halo_send, halo_recv, rs_send, rs_recv, ag_send, ag_recv, sm_send, sm_recv,
):
    rows, cols, chans = COT.shape
    me = lax.axis_index("tile")
    bits = count.bit_length() - 1
    half = count // 2
    right = (me + 1) % count
    left = (me + count - 1) % count
    across = (me + half) % count
    across_right = (me + half + 1) % count
    across_left = (me + half - 1) % count

    def bit_of(b):
        return (me // (1 << b)) % 2

    def peer(b):
        return me + (1 - 2 * bit_of(b)) * (1 << b)

    def remote(src, dst, send, recv, target):
        return pltpu.make_async_remote_copy(
            src_ref=src, dst_ref=dst, send_sem=send, recv_sem=recv,
            device_id={"tile": target}, device_id_type=pl.DeviceIdType.MESH,
        )

    load_f = pltpu.make_async_copy(fields_hbm, F.at[pl.ds(1, rows)], load_sem.at[0])
    load_c = pltpu.make_async_copy(cot_hbm, COT, load_sem.at[1])
    load_o = pltpu.make_async_copy(w_out_hbm, WO, load_sem.at[2])
    load_i = pltpu.make_async_copy(w_in_hbm, WI, load_sem.at[3])
    load_f.start()
    load_c.start()
    load_o.start()
    load_i.start()

    friends = [right, left, across, across_right, across_left] + [peer(b) for b in range(bits - 1)]
    barrier = pltpu.get_barrier_semaphore()
    for friend in friends:
        pl.semaphore_signal(barrier, inc=1, device_id={"tile": friend}, device_id_type=pl.DeviceIdType.MESH)
    pl.semaphore_wait(barrier, len(friends))

    lane_chunks = [pl.ds(c * LANES, LANES) for c in range(chans // LANES)]
    spot = lax.broadcasted_iota(jnp.int32, (cols, LANES), 0)
    first = spot == 0
    last = spot == cols - 1

    def send_halo(ext, base):
        copies = [
            remote(ext.at[1], ext.at[0], halo_send.at[base], halo_recv.at[base], across),
            remote(ext.at[rows], ext.at[rows + 1], halo_send.at[base + 1], halo_recv.at[base + 1], across),
        ]
        slot = 0 if base == 0 else 2
        for copy in copies:
            copy.start()
        for side in range(2):
            def rounded(t, _):
                at = pl.ds(pl.multiple_of(t * 16, 16), 16)
                CS[slot + side, at, :] = COL[side, at, :].astype(BF16)
                return 0
            lax.fori_loop(0, rows // 16, rounded, 0)
            ends = jnp.concatenate([COL[side, 0:8, :], COL[side, rows - 8 : rows, :]], axis=0)
            KS[slot + side] = ends.astype(BF16)
        more = [
            remote(CS.at[slot + 1], CR.at[slot], halo_send.at[base + 2], halo_recv.at[base + 2], right),
            remote(CS.at[slot], CR.at[slot + 1], halo_send.at[base + 3], halo_recv.at[base + 3], left),
            remote(KS.at[slot + 1], KR.at[slot], halo_send.at[base + 4], halo_recv.at[base + 4], across_right),
            remote(KS.at[slot], KR.at[slot + 1], halo_send.at[base + 5], halo_recv.at[base + 5], across_left),
        ]
        for copy in more:
            copy.start()
        return copies + more

    def widen_halo(slot):
        for side in range(2):
            def opened(t, _):
                at = pl.ds(pl.multiple_of(t * 16, 16), 16)
                HX[side, pl.ds(pl.multiple_of(8 + t * 16, 8), 16), :] = CR[slot + side, at, :].astype(F32)
                return 0
            lax.fori_loop(0, rows // 16, opened, 0)
            ends = KR[slot + side].astype(F32)
            HX[side, 7:8, :] = ends[0:1]
            HX[side, 8 + rows : 9 + rows, :] = ends[15:16]

    load_f.wait()

    def take_columns(i, _):
        row = F[i + 1].astype(F32)
        COL[0, pl.ds(i, 1), :] = row[0:1]
        COL[1, pl.ds(i, 1), :] = row[cols - 1 : cols]
        return 0
    lax.fori_loop(0, rows, take_columns, 0)
    halo = send_halo(F, 0)

    load_c.wait()
    load_o.wait()
    load_i.wait()
    step = 16
    blocks = rows // step

    def hidden_grad(k, _):
        at = pl.ds(k * step, step)
        up = COT[at].reshape(step * cols, chans)
        for lanes in lane_chunks:
            GH[at, :, lanes] = lax.dot_general(
                up, WO[lanes, :], NT, preferred_element_type=F32
            ).reshape(step, cols, LANES)
        return 0
    lax.fori_loop(0, blocks, hidden_grad, 0)

    for copy in halo:
        copy.wait()
    widen_halo(0)
    for lanes in lane_chunks:
        for side in range(2):
            total = taps[2 * side : 2 * side + 1, lanes] * HX[side, 7 : 7 + rows, lanes]
            for a in range(1, 3):
                t = 3 * a + 2 * side
                total = total + taps[t : t + 1, lanes] * HX[side, 7 + a : 7 + a + rows, lanes]
            EDGE[side, :, lanes] = total

    def forward(k, _):
        def norm_row(q, _):
            i = k * step + q
            squares = jnp.zeros((cols, 128), F32)
            ground = land[i]
            for lanes in lane_chunks:
                window = [F[i + a, :, lanes].astype(F32) for a in range(3)]
                sums = []
                for b in range(3):
                    s = taps[b : b + 1, lanes] * window[0]
                    for a in range(1, 3):
                        s = s + taps[3 * a + b : 3 * a + b + 1, lanes] * window[a]
                    sums.append(s)
                depth = sums[1]
                depth = depth + jnp.where(first, EDGE[0, pl.ds(i, 1), lanes], pltpu.roll(sums[0], 1, 0))
                depth = depth + jnp.where(last, EDGE[1, pl.ds(i, 1), lanes], pltpu.roll(sums[2], cols - 1, 0))
                depth = depth + jnp.concatenate([ground] * (LANES // 128), axis=1) * bias[0:1, lanes]
                D[i, :, lanes] = depth
                for part in range(LANES // 128):
                    piece = depth[:, part * 128 : (part + 1) * 128]
                    squares = squares + piece * piece
            mean = jnp.sum(squares, axis=1, keepdims=True) * (1.0 / chans)
            scale = lax.rsqrt(mean + EPS)
            SC[i] = jnp.broadcast_to(scale, (cols, 128))
            for lanes in lane_chunks:
                NRM[i, :, lanes] = (D[i, :, lanes] * scale * gain[0:1, lanes]).astype(BF16)
            return 0
        lax.fori_loop(0, step, norm_row, 0)
        normed = NRM[pl.ds(k * step, step)].reshape(step * cols, chans)
        for lanes in lane_chunks:
            PRE[:, :, lanes] = jnp.dot(
                normed, WI[:, lanes], preferred_element_type=F32
            ).reshape(step, cols, LANES)

        def gelu_row(q, _):
            i = k * step + q
            for lanes in lane_chunks:
                pre = PRE[q, :, lanes]
                cdf = 0.5 * (1.0 + lax.erf(pre * INV_ROOT_TWO))
                slope = cdf + pre * jnp.exp(-0.5 * pre * pre) * INV_ROOT_TWO_PI
                HID[i, :, lanes] = (pre * cdf).astype(BF16)
                GP[i, :, lanes] = (GH[i, :, lanes] * slope).astype(BF16)
            return 0
        lax.fori_loop(0, step, gelu_row, 0)
        return 0
    lax.fori_loop(0, blocks, forward, 0)

    core = bit_of(0)
    mid = chans // 2
    keep0 = pl.multiple_of(core * mid, mid)
    send0 = pl.multiple_of((1 - core) * mid, mid)

    def weight_grad(w, lhs, rhs, base):
        def chunk(t, _):
            at = pl.ds(pl.multiple_of(base + t * LANES, LANES), LANES)
            left_side = lhs[:, :, at].reshape(rows * cols, LANES)
            for lanes in lane_chunks:
                right_side = rhs[:, :, lanes].reshape(rows * cols, LANES)
                G[w, at, lanes] = lax.dot_general(
                    left_side, right_side, TN, preferred_element_type=F32
                ).astype(BF16)
            return 0
        lax.fori_loop(0, mid // LANES, chunk, 0)

    def swap_core(w):
        copy = remote(G.at[w, pl.ds(send0, mid)], RB.at[w], rs_send.at[w], rs_recv.at[w], peer(0))
        copy.start()
        return copy

    def fold(w, base, size, source, offset):
        def add(t, _):
            at = pl.ds(pl.multiple_of(base + t * 16, 16), 16)
            come = source[pl.ds(pl.multiple_of(offset + t * 16, 16), 16), :]
            G[w, at, :] = (G[w, at, :].astype(F32) + come.astype(F32)).astype(BF16)
            return 0
        lax.fori_loop(0, size // 16, add, 0)

    middle = list(range(1, bits - 1))
    pieces = mid // 2
    orders = []
    bases = []
    for p in range(4):
        turn = p % len(middle)
        orders.append(middle[turn:] + middle[:turn] + [bits - 1])
        bases.append([keep0 + (p % 2) * pieces])
    stages = bits - 1
    offsets = [pieces - (pieces >> s) for s in range(stages)]

    def rs_start(p, s):
        size = pieces >> (s + 1)
        b = orders[p][s]
        base = bases[p][s]
        away = pl.multiple_of(base + (1 - bit_of(b)) * size, 16)
        bases[p].append(base + bit_of(b) * size)
        n = 2 + p * stages + s
        copy = remote(
            G.at[p // 2, pl.ds(away, size)], RP.at[p, pl.ds(offsets[s], size)],
            rs_send.at[n], rs_recv.at[n], peer(b),
        )
        copy.start()
        return copy

    def rs_finish(copy, p, s):
        copy.wait()
        fold(p // 2, bases[p][s + 1], pieces >> (s + 1), RP.at[p], offsets[s])

    def ag_start(p, s):
        size = pieces >> (s + 1)
        at = pl.ds(pl.multiple_of(bases[p][s + 1], 16), size)
        b = orders[p][s] if s >= 0 else 0
        n = p * bits + s + 1
        copy = remote(A.at[p // 2, at], A.at[p // 2, at], ag_send.at[n], ag_recv.at[n], peer(b))
        copy.start()
        return copy

    flight = {}

    def advance(p):
        state, copy = flight[p]
        if state[0] == "rs":
            s = state[1]
            rs_finish(copy, p, s)
            if s + 1 < stages:
                flight[p] = (("rs", s + 1), rs_start(p, s + 1))
            else:
                at = pl.ds(pl.multiple_of(bases[p][stages], 16), pieces >> stages)
                A[p // 2, at, :] = G[p // 2, at, :]
                flight[p] = (("ag", stages - 1), ag_start(p, stages - 1))
        elif state[0] == "ag":
            s = state[1]
            copy.wait()
            if s >= 0:
                flight[p] = (("ag", s - 1), ag_start(p, s - 1))
            else:
                flight[p] = (("done",), None)

    weight_grad(0, HID, COT, send0)
    core0 = swap_core(0)
    weight_grad(0, HID, COT, keep0)
    core0.wait()
    fold(0, keep0, mid, RB.at[0], 0)
    for p in (0, 1):
        flight[p] = (("rs", 0), rs_start(p, 0))
    weight_grad(1, NRM, GP, send0)
    core1 = swap_core(1)
    weight_grad(1, NRM, GP, keep0)
    core1.wait()
    fold(1, keep0, mid, RB.at[1], 0)
    for p in (2, 3):
        flight[p] = (("rs", 0), rs_start(p, 0))
    for p in (0, 1):
        advance(p)

    GA[...] = jnp.zeros_like(GA)
    LA[...] = jnp.zeros_like(LA)

    def backward(k, _):
        at = pl.ds(k * step, step)
        g_pre = GP[at].reshape(step * cols, chans)
        for lanes in lane_chunks:
            GH[at, :, lanes] = lax.dot_general(
                g_pre, WI[lanes, :], NT, preferred_element_type=F32
            ).reshape(step, cols, LANES)

        def norm_row(q, _):
            i = k * step + q
            scale = SC[i]
            wide = jnp.concatenate([scale] * (LANES // 128), axis=1)
            ground = jnp.concatenate([land[i]] * (LANES // 128), axis=1)
            inner = jnp.zeros((cols, 128), F32)
            for lanes in lane_chunks:
                g = GH[i, :, lanes]
                product = g * D[i, :, lanes]
                GA[:, lanes] = GA[:, lanes] + product * wide
                weighted = product * gain[0:1, lanes]
                for part in range(LANES // 128):
                    inner = inner + weighted[:, part * 128 : (part + 1) * 128]
            mean = jnp.sum(inner, axis=1, keepdims=True) * (1.0 / chans)
            cube = scale * scale * scale * mean
            cube = jnp.concatenate([cube] * (LANES // 128), axis=1)
            for lanes in lane_chunks:
                g = wide * (GH[i, :, lanes] * gain[0:1, lanes]) - D[i, :, lanes] * cube
                rounded = g.astype(BF16)
                GX[i + 1, :, lanes] = rounded
                g = rounded.astype(F32)
                LA[:, lanes] = LA[:, lanes] + g * ground
                COL[0, pl.ds(i, 1), lanes] = g[0:1]
                COL[1, pl.ds(i, 1), lanes] = g[cols - 1 : cols]
            return 0
        lax.fori_loop(0, step, norm_row, 0)
        return 0

    cut = blocks // 2
    lax.fori_loop(0, cut, backward, 0)
    for p in range(4):
        advance(p)
    lax.fori_loop(cut, blocks, backward, 0)
    g_halo = send_halo(GX, 6)
    for p in range(4):
        advance(p)

    zero = jnp.zeros((8, LANES), F32)
    for c, lanes in enumerate(lane_chunks):
        def tap_row(i, sums):
            g = GX[i + 1, :, lanes].astype(F32)
            sides = [
                jnp.where(last, 0.0, pltpu.roll(g, cols - 1, 0)),
                g,
                jnp.where(first, 0.0, pltpu.roll(g, 1, 0)),
            ]
            new = []
            for a in range(3):
                row = F[i + a, :, lanes].astype(F32)
                for b in range(3):
                    product = sides[b] * row
                    piece = product[0:8]
                    for top in range(8, cols, 8):
                        piece = piece + product[top : top + 8]
                    new.append(sums[3 * a + b] + piece)
            return tuple(new)
        sums = list(lax.fori_loop(0, rows, tap_row, (zero,) * 9))
        lines = []
        for a in range(3):
            for b in range(3):
                line = jnp.sum(sums[3 * a + b], axis=0, keepdims=True)
                if b != 1:
                    side = b // 2
                    line = line + jnp.sum(
                        COL[side, :, lanes] * HX[side, 7 + a : 7 + a + rows, lanes], axis=0, keepdims=True
                    )
                lines.append(line)
        lines.append(jnp.sum(GA[:, lanes], axis=0, keepdims=True))
        lines.append(jnp.sum(LA[:, lanes], axis=0, keepdims=True))
        lines.append(jnp.zeros((5, LANES), F32))
        SS[0, :, lanes] = jnp.concatenate(lines, axis=0)
        advance(c % 4)

    def small_start(b):
        copy = remote(SS.at[b], SR.at[b], sm_send.at[b], sm_recv.at[b], peer(b))
        copy.start()
        return copy

    def small_finish(copy, b):
        copy.wait()
        SS[b + 1] = SS[b] + SR[b]

    small = small_start(0)
    for copy in g_halo:
        copy.wait()
    widen_halo(2)
    for lanes in lane_chunks:
        for side in range(2):
            north = HX[side, 7:8, lanes]
            south = HX[side, 8 + rows : 9 + rows, lanes]
            near = 2 - 2 * side
            middle_rows = taps[3 + near : 4 + near, lanes] * HX[side, 8 : 8 + rows, lanes]
            above = taps[6 + near : 7 + near, lanes] * HX[side, 7 : 7 + rows, lanes]
            below = taps[near : near + 1, lanes] * HX[side, 9 : 9 + rows, lanes]
            line = lax.broadcasted_iota(jnp.int32, (rows, LANES), 0)
            above = jnp.where(line == 0, taps[near : near + 1, lanes] * north, above)
            below = jnp.where(line == rows - 1, taps[6 + near : 7 + near, lanes] * south, below)
            EDGE[side, :, lanes] = middle_rows + above + below

    def spread_row(i, top, bottom):
        for lanes in lane_chunks:
            above = GX[i, :, lanes].astype(F32)
            here = GX[i + 1, :, lanes].astype(F32)
            below = GX[i + 2, :, lanes].astype(F32)
            sums = []
            for b in range(3):
                s = taps[3 * top + b : 3 * top + b + 1, lanes] * above
                s = s + taps[3 + b : 4 + b, lanes] * here
                s = s + taps[3 * bottom + b : 3 * bottom + b + 1, lanes] * below
                sums.append(s)
            total = sums[1] + COT[i, :, lanes].astype(F32)
            total = total + jnp.where(last, EDGE[1, pl.ds(i, 1), lanes], pltpu.roll(sums[0], cols - 1, 0))
            total = total + jnp.where(first, EDGE[0, pl.ds(i, 1), lanes], pltpu.roll(sums[2], 1, 0))
            HID[i, :, lanes] = total.astype(BF16)

    def spread(i, _):
        spread_row(i, 2, 0)
        return 0

    spread_row(0, 0, 0)
    spread_row(rows - 1, 2, 2)
    legs = bits
    edges = [1 + (rows - 2) * t // legs for t in range(legs + 1)]
    for t in range(legs):
        lax.fori_loop(edges[t], edges[t + 1], spread, 0)
        small_finish(small, t)
        if t + 1 < bits:
            small = small_start(t + 1)
        for p in range(4):
            advance(p)
    store = pltpu.make_async_copy(HID, out_hbm, load_sem.at[0])
    store.start()
    for _ in range(2 * bits):
        for p in range(4):
            advance(p)
    small_out[...] = SS[bits]
    save = pltpu.make_async_copy(A, gw_hbm, load_sem.at[1])
    save.start()
    store.wait()
    save.wait()


def body(fields, kernel, norm_gain, land_bias, w_in, w_out, land_mask, cotangent):
    rows, cols, chans = fields.shape
    count = lax.axis_size("tile")
    bits = count.bit_length() - 1
    land = jnp.broadcast_to(land_mask.astype(F32)[:, :, None], (rows, cols, 128))
    vm = pltpu.VMEM
    grid3 = (rows, cols, chans)
    dma = pltpu.SemaphoreType.DMA
    anywhere = pl.BlockSpec(memory_space=pl.ANY)
    inside = pl.BlockSpec(memory_space=pltpu.VMEM)
    pieces = chans // 4
    out, gw, small = pl.pallas_call(
        functools.partial(block_kernel, count),
        out_shape=(
            jax.ShapeDtypeStruct(grid3, BF16),
            jax.ShapeDtypeStruct((2, chans, chans), BF16),
            jax.ShapeDtypeStruct((16, chans), F32),
        ),
        in_specs=[anywhere] * 4 + [inside] * 4,
        out_specs=(anywhere, anywhere, inside),
        scratch_shapes=[
            vm((rows + 2, cols, chans), BF16),
            vm(grid3, BF16),
            vm((chans, chans), BF16),
            vm((chans, chans), BF16),
            vm(grid3, F32),
            vm(grid3, BF16),
            vm(grid3, F32),
            vm(grid3, BF16),
            vm(grid3, BF16),
            vm((rows + 2, cols, chans), BF16),
            vm((16, cols, chans), F32),
            vm((rows, cols, 128), F32),
            vm((2, chans, chans), BF16),
            vm((2, chans // 2, chans), BF16),
            vm((4, pieces, chans), BF16),
            vm((2, chans, chans), BF16),
            vm((2, rows, chans), F32),
            vm((2, rows + 16, chans), F32),
            vm((2, rows, chans), F32),
            vm((4, rows, chans), BF16),
            vm((4, rows, chans), BF16),
            vm((4, 16, chans), BF16),
            vm((4, 16, chans), BF16),
            vm((cols, chans), F32),
            vm((cols, chans), F32),
            vm((bits + 1, 16, chans), F32),
            vm((bits, 16, chans), F32),
            dma((4,)),
            dma((12,)),
            dma((12,)),
            dma((2 + 4 * (bits - 1),)),
            dma((2 + 4 * (bits - 1),)),
            dma((4 * bits,)),
            dma((4 * bits,)),
            dma((bits,)),
            dma((bits,)),
        ],
        compiler_params=pltpu.CompilerParams(
            collective_id=0, has_side_effects=True, vmem_limit_bytes=62 * 1024 * 1024
        ),
    )(fields, cotangent, w_in, w_out, kernel, norm_gain[None], land_bias[None], land)
    wide = gw.astype(F32)
    return (out, wide[1], wide[0], small[:9], small[9], small[10])


def solution(mesh):
    placed = (
        P("groups", "tile", None),
        P(),
        P(),
        P(),
        P(),
        P(),
        P("groups", "tile"),
        P("groups", "tile", None),
    )
    return jax.shard_map(
        body,
        mesh=mesh,
        in_specs=placed,
        out_specs=(
            P("groups", "tile", None),
            P("groups", None),
            P("groups", None),
            P("groups", None),
            P("groups"),
            P("groups"),
        ),
        check_vma=False,
    )
```

time: 280 us -> 132 us (0.47)
  Pallas kernels: 0 us -> 119 us
  waiting for transfers between devices: 104 us -> 0 us
  other arithmetic: 70.7 us -> 3.91 us
  blocking collectives: 40.1 us -> 0 us
  matrix products: 24.7 us -> 0 us
  between operations: 14.5 us -> 0.67 us
  starting transfers between devices: 9.95 us -> 0 us
  local copies, waits for them, and re-layouts: 15.5 us -> 8.42 us
    pallas_call x0 -> x1, Pallas kernels: none -> 119 us  [body(): pl.pallas_call(functools.partial(block_kernel, count), out_shape=(jax.Sha...]
    psum x1 -> x0, waiting for transfers between devices: 90.2 us -> none  [body(): lax.psum((grad_w_in, grad_w_out, grad_kernel, grad_gain, grad_land), 'tile')]
    reduce_sum x3 -> x0, other arithmetic: 40.9 us -> none  [the longest x1 24.3 us: body(): tap_terms.append(jnp.sum(g_float * window, axis=(0, 1)))]
    psum x1 -> x0, blocking collectives: 40.1 us -> none  [body(): lax.psum((grad_w_in, grad_w_out, grad_kernel, grad_gain, grad_land), 'tile')]
    dot_general x5 -> x0, matrix products: 24.7 us -> none  [the longest x1 5.49 us: body(): g_hidden = jnp.dot(upstream, w_out.T, preferred_element_type=jnp.float32)]
    concatenate x2 -> x0, other arithmetic: 16 us -> none  [the longest x1 11 us: body(): padded = jnp.concatenate([partner[:1], widened, partner[1:]], axis=0)]
    ppermute x6 -> x0, waiting for transfers between devices: 13.7 us -> none  [the longest x2 5.35 us: swapped(): return lax.ppermute(block, axis, route)]
    ppermute x6 -> x0, starting transfers between devices: 9.91 us -> none  [the longest x2 7.12 us: extended(): lax.ppermute(head, axis, [((i + 1) % count, i) for i in range(count)])]
  transfers between devices with their start and end apart: 7 -> 0, of which waited for: 4 -> 0; matrix products, arithmetic and copies ran while one was open for 16% -> 0% of each run, Pallas kernels for 0% -> 0%
where the time goes in v1:
time: 132 us
  Pallas kernels  119 us (90%)
  local copies, waits for them, and re-layouts  8.42 us (6%)
  other arithmetic  3.91 us (3%)
    pallas_call x1, Pallas kernels, body(): pl.pallas_call(functools.partial(block_kernel, count), out_shape=(jax.Sha...  119 us
    squeeze x1, local copies, waits for them, and re-layouts, body(): return (out, wide[1], wide[0], small[:9], small[9], small[10])  4.27 us
    convert_element_type x1, other arithmetic, body(): wide = gw.astype(F32)  3.21 us

profile of v1, /device:TPU:0, one launch (start us, length us, event | category | flops | bytes accessed | tf_op | source)
XLA Modules:
  0.0 131.8 jit_solution(10143411258388482685)
XLA Ops:
  0.6 0.7 convert_element_type.6
  1.3 0.1 copy.14
  1.4 1.1 broadcast_in_dim.14.land
  2.6 118.8 %shard_map.127 = (bf16[96,16,1024]{2,1,0:T(8,128)(2,1)}, bf16[2,1024,1024]{2,1,0:T(8,128)(2,1)}, f32[16,1024]{1,0:T(8,128)}) custom-call(bf16[96,16,1024]{2,1,0:T(8,128)(2,1)} %fields_hbm.1, bf16[96,16,1024]{2,1,0:T(8,128)(2,1)} %cot_hbm.1, bf16[1024,1024]{1,0:T(8,128)(2,1)} %w_in_hbm.1, bf16[1024,1024]{1,0:T(8,128)(2,1)} %w_out_hbm.1, f32[9,1024]{1,0:T(8,128)} %taps.1, ...), custom_call_target="tpu_custom_call" | custom-call | tf_op jit(solution)/shard_map/pallas_call | solution.py:460
  121.4 3.2 %convert_element_type.7 = f32[2,1024,1024]{2,1,0:T(8,128)S(1)} convert(bf16[2,1024,1024]{2,1,0:T(8,128)(2,1)} %get-tuple-element.10) | non-fusion elementwise | flops 2097152 | bytes 12582912 | tf_op jit(solution)/shard_map/convert_element_type | solution.py:511
  124.6 0.0 copy-start.1
  124.6 0.0 copy-start
  124.7 4.3 %slice_bitcast_fusion = (f32[1024,1024]{1,0:T(8,128)}, f32[1024,1024]{1,0:T(8,128)}) fusion(f32[2,1024,1024]{2,1,0:T(8,128)S(1)} %convert_element_type.7), kind=kLoop, calls=%fused_computation | loop fusion | bytes 16777216 | tf_op jit(solution)/shard_map/squeeze | solution.py:512
  128.9 0.0 copy-done.1
  128.9 0.6 fusion
  129.5 0.0 copy-done
  129.5 1.7 %copy.17 = bf16[96,16,1024]{2,1,0:T(8,128)(2,1)} copy(bf16[96,16,1024]{2,1,0:T(8,128)(2,1)S(1)} %copy-done) | data formatting | bytes 6291456
  131.2 0.6 copy.18
Async XLA Ops:
  124.6 4.3 %copy-start.1 = (f32[16,1024]{1,0:T(8,128)S(1)}, f32[16,1024]{1,0:T(8,128)}, u32[]{:S(2)}) copy-start(f32[16,1024]{1,0:T(8,128)} %get-tuple-element.11) | copy-start | bytes 196612
  124.6 4.9 %copy-start = (bf16[96,16,1024]{2,1,0:T(8,128)(2,1)S(1)}, bf16[96,16,1024]{2,1,0:T(8,128)(2,1)}, u32[]{:S(2)}) copy-start(bf16[96,16,1024]{2,1,0:T(8,128)(2,1)} %get-tuple-element.22) | copy-start | bytes 9437188

commit v2 on v1

--- a/solution.py
+++ b/solution.py
@@ -19,8 +19,8 @@
 
 def block_kernel(
     count, fields_hbm, cot_hbm, w_in_hbm, w_out_hbm, taps, gain, bias, land,
-    out_hbm, gw_hbm, small_out,
-    F, COT, WI, WO, D, NRM, GH, HID, GP, GX, PRE, SC, G, RB, RP, A,
+    out_hbm, gw_out_hbm, gw_in_hbm, small_out,
+    F, COT, WI, WO, D, NRM, GH, HID, GP, GX, PRE, SC, SQ, G, RB, RP, A,
     COL, HX, EDGE, CS, CR, KS, KR, GA, LA, SS, SR,
     load_sem, halo_send, halo_recv, rs_send, rs_recv, ag_send, ag_recv, sm_send, sm_recv,
 ):
@@ -141,7 +141,7 @@
             EDGE[side, :, lanes] = total
 
     def forward(k, _):
-        def norm_row(q, _):
+        def depth_row(q, _):
             i = k * step + q
             squares = jnp.zeros((cols, 128), F32)
             ground = land[i]
@@ -161,13 +161,19 @@
                 for part in range(LANES // 128):
                     piece = depth[:, part * 128 : (part + 1) * 128]
                     squares = squares + piece * piece
-            mean = jnp.sum(squares, axis=1, keepdims=True) * (1.0 / chans)
-            scale = lax.rsqrt(mean + EPS)
-            SC[i] = jnp.broadcast_to(scale, (cols, 128))
+            SQ[q] = squares
+            return 0
+        lax.fori_loop(0, step, depth_row, 0, unroll=2)
+        mean = jnp.sum(SQ[...], axis=2, keepdims=True) * (1.0 / chans)
+        SC[pl.ds(k * step, step)] = jnp.broadcast_to(lax.rsqrt(mean + EPS), (step, cols, 128))
+
+        def norm_row(q, _):
+            i = k * step + q
+            wide = jnp.concatenate([SC[i]] * (LANES // 128), axis=1)
             for lanes in lane_chunks:
-                NRM[i, :, lanes] = (D[i, :, lanes] * scale * gain[0:1, lanes]).astype(BF16)
-            return 0
-        lax.fori_loop(0, step, norm_row, 0)
+                NRM[i, :, lanes] = (D[i, :, lanes] * wide * gain[0:1, lanes]).astype(BF16)
+            return 0
+        lax.fori_loop(0, step, norm_row, 0, unroll=2)
         normed = NRM[pl.ds(k * step, step)].reshape(step * cols, chans)
         for lanes in lane_chunks:
             PRE[:, :, lanes] = jnp.dot(
@@ -183,7 +189,7 @@
                 HID[i, :, lanes] = (pre * cdf).astype(BF16)
                 GP[i, :, lanes] = (GH[i, :, lanes] * slope).astype(BF16)
             return 0
-        lax.fori_loop(0, step, gelu_row, 0)
+        lax.fori_loop(0, step, gelu_row, 0, unroll=2)
         return 0
     lax.fori_loop(0, blocks, forward, 0)
 
@@ -304,11 +310,9 @@
                 g_pre, WI[lanes, :], NT, preferred_element_type=F32
             ).reshape(step, cols, LANES)
 
-        def norm_row(q, _):
+        def inner_row(q, _):
             i = k * step + q
-            scale = SC[i]
-            wide = jnp.concatenate([scale] * (LANES // 128), axis=1)
-            ground = jnp.concatenate([land[i]] * (LANES // 128), axis=1)
+            wide = jnp.concatenate([SC[i]] * (LANES // 128), axis=1)
             inner = jnp.zeros((cols, 128), F32)
             for lanes in lane_chunks:
                 g = GH[i, :, lanes]
@@ -317,9 +321,18 @@
                 weighted = product * gain[0:1, lanes]
                 for part in range(LANES // 128):
                     inner = inner + weighted[:, part * 128 : (part + 1) * 128]
-            mean = jnp.sum(inner, axis=1, keepdims=True) * (1.0 / chans)
-            cube = scale * scale * scale * mean
-            cube = jnp.concatenate([cube] * (LANES // 128), axis=1)
+            SQ[q] = inner
+            return 0
+        lax.fori_loop(0, step, inner_row, 0, unroll=2)
+        mean = jnp.sum(SQ[...], axis=2, keepdims=True) * (1.0 / chans)
+        scales = SC[at]
+        SQ[...] = scales * scales * scales * mean
+
+        def depth_grad_row(q, _):
+            i = k * step + q
+            wide = jnp.concatenate([SC[i]] * (LANES // 128), axis=1)
+            cube = jnp.concatenate([SQ[q]] * (LANES // 128), axis=1)
+            ground = jnp.concatenate([land[i]] * (LANES // 128), axis=1)
             for lanes in lane_chunks:
                 g = wide * (GH[i, :, lanes] * gain[0:1, lanes]) - D[i, :, lanes] * cube
                 rounded = g.astype(BF16)
@@ -329,14 +342,17 @@
                 COL[0, pl.ds(i, 1), lanes] = g[0:1]
                 COL[1, pl.ds(i, 1), lanes] = g[cols - 1 : cols]
             return 0
-        lax.fori_loop(0, step, norm_row, 0)
+        lax.fori_loop(0, step, depth_grad_row, 0, unroll=2)
         return 0
 
-    cut = blocks // 2
-    lax.fori_loop(0, cut, backward, 0)
+    cuts = [blocks * t // 3 for t in range(4)]
+    lax.fori_loop(cuts[0], cuts[1], backward, 0)
     for p in range(4):
         advance(p)
-    lax.fori_loop(cut, blocks, backward, 0)
+    lax.fori_loop(cuts[1], cuts[2], backward, 0)
+    for p in range(4):
+        advance(p)
+    lax.fori_loop(cuts[2], cuts[3], backward, 0)
     g_halo = send_halo(GX, 6)
     for p in range(4):
         advance(p)
@@ -360,7 +376,7 @@
                         piece = piece + product[top : top + 8]
                     new.append(sums[3 * a + b] + piece)
             return tuple(new)
-        sums = list(lax.fori_loop(0, rows, tap_row, (zero,) * 9))
+        sums = list(lax.fori_loop(0, rows, tap_row, (zero,) * 9, unroll=2))
         lines = []
         for a in range(3):
             for b in range(3):
@@ -375,7 +391,9 @@
         lines.append(jnp.sum(LA[:, lanes], axis=0, keepdims=True))
         lines.append(jnp.zeros((5, LANES), F32))
         SS[0, :, lanes] = jnp.concatenate(lines, axis=0)
-        advance(c % 4)
+        if c % 2 == 1:
+            for p in range(4):
+                advance(p)
 
     def small_start(b):
         copy = remote(SS.at[b], SR.at[b], sm_send.at[b], sm_recv.at[b], peer(b))
@@ -440,10 +458,13 @@
         for p in range(4):
             advance(p)
     small_out[...] = SS[bits]
-    save = pltpu.make_async_copy(A, gw_hbm, load_sem.at[1])
-    save.start()
+    save_out = pltpu.make_async_copy(A.at[0], gw_out_hbm, load_sem.at[1])
+    save_in = pltpu.make_async_copy(A.at[1], gw_in_hbm, load_sem.at[2])
+    save_out.start()
+    save_in.start()
     store.wait()
-    save.wait()
+    save_out.wait()
+    save_in.wait()
 
 
 def body(fields, kernel, norm_gain, land_bias, w_in, w_out, land_mask, cotangent):
@@ -457,15 +478,16 @@
     anywhere = pl.BlockSpec(memory_space=pl.ANY)
     inside = pl.BlockSpec(memory_space=pltpu.VMEM)
     pieces = chans // 4
-    out, gw, small = pl.pallas_call(
+    out, gw_out, gw_in, small = pl.pallas_call(
         functools.partial(block_kernel, count),
         out_shape=(
             jax.ShapeDtypeStruct(grid3, BF16),
-            jax.ShapeDtypeStruct((2, chans, chans), BF16),
+            jax.ShapeDtypeStruct((chans, chans), BF16),
+            jax.ShapeDtypeStruct((chans, chans), BF16),
             jax.ShapeDtypeStruct((16, chans), F32),
         ),
         in_specs=[anywhere] * 4 + [inside] * 4,
-        out_specs=(anywhere, anywhere, inside),
+        out_specs=(anywhere, anywhere, anywhere, inside),
         scratch_shapes=[
             vm((rows + 2, cols, chans), BF16),
             vm(grid3, BF16),
@@ -479,6 +501,7 @@
             vm((rows + 2, cols, chans), BF16),
             vm((16, cols, chans), F32),
             vm((rows, cols, 128), F32),
+            vm((16, cols, 128), F32),
             vm((2, chans, chans), BF16),
             vm((2, chans // 2, chans), BF16),
             vm((4, pieces, chans), BF16),
@@ -508,8 +531,7 @@
             collective_id=0, has_side_effects=True, vmem_limit_bytes=62 * 1024 * 1024
         ),
     )(fields, cotangent, w_in, w_out, kernel, norm_gain[None], land_bias[None], land)
-    wide = gw.astype(F32)
-    return (out, wide[1], wide[0], small[:9], small[9], small[10])
+    return (out, gw_in.astype(F32), gw_out.astype(F32), small[:9], small[9], small[10])
 
 
 def solution(mesh):

time: 132 us -> 123 us (0.932)
  Pallas kernels: 119 us -> 110 us
  local copies, waits for them, and re-layouts: 8.42 us -> 4.22 us
  other arithmetic: 3.91 us -> 7.4 us
    pallas_call x1, Pallas kernels: 119 us -> 110 us  [body(): pl.pallas_call(functools.partial(block_kernel, count), out_shape=(jax.Sha...]
    squeeze x1 -> x0, local copies, waits for them, and re-layouts: 4.27 us -> none  [body(): return (out, wide[1], wide[0], small[:9], small[9], small[10])]
    convert_element_type x1 -> x2, other arithmetic: 3.21 us -> 6.7 us  [the longest x1 4.22 us: body(): gw_in.astype(F32)]
where the time goes in v2:
time: 123 us; the launch traced here: 122 us
  Pallas kernels  110 us (89%)
  other arithmetic  7.4 us (6%)
  local copies, waits for them, and re-layouts  4.22 us (3%)
    pallas_call x1, Pallas kernels, body(): pl.pallas_call(functools.partial(block_kernel, count), out_shape=(jax.Sha...  110 us
    convert_element_type x1, other arithmetic, body(): gw_in.astype(F32)  4.22 us
    convert_element_type x1, other arithmetic, body(): gw_out.astype(F32)  2.48 us

profile of v2, /device:TPU:0, one launch (start us, length us, event | category | flops | bytes accessed | tf_op | source)
XLA Modules:
  0.0 122.4 jit_solution(14811729040779787142)
XLA Ops:
  0.6 0.7 convert_element_type.9
  1.3 0.1 copy.14
  1.4 1.1 broadcast_in_dim.14.land
  2.6 110.1 %shard_map.127 = (bf16[96,16,1024]{2,1,0:T(8,128)(2,1)}, bf16[1024,1024]{1,0:T(8,128)(2,1)}, bf16[1024,1024]{1,0:T(8,128)(2,1)}, f32[16,1024]{1,0:T(8,128)}) custom-call(bf16[96,16,1024]{2,1,0:T(8,128)(2,1)} %fields_hbm.1, bf16[96,16,1024]{2,1,0:T(8,128)(2,1)} %cot_hbm.1, bf16[1024,1024]{1,0:T(8,128)(2,1)} %w_in_hbm.1, bf16[1024,1024]{1,0:T(8,128)(2,1)} %w_out_hbm.1, ...), custom_call_target="tpu_custom_call" | custom-call | tf_op jit(solution)/shard_map/pallas_call | solution.py:481
  112.7 0.0 copy-start.1
  112.7 4.2 %convert_element_type.10 = f32[1024,1024]{1,0:T(8,128)} convert(bf16[1024,1024]{1,0:T(8,128)(2,1)} %get-tuple-element.11) | non-fusion elementwise | flops 1048576 | bytes 6291456 | tf_op jit(solution)/shard_map/convert_element_type | solution.py:534
  116.9 0.0 copy-done.1
  116.9 0.0 copy-start.2
  116.9 0.0 copy-start
  116.9 2.5 %convert_element_type.11 = f32[1024,1024]{1,0:T(8,128)} convert(bf16[1024,1024]{1,0:T(8,128)(2,1)S(1)} %copy-done.1) | non-fusion elementwise | flops 1048576 | bytes 6291456 | tf_op jit(solution)/shard_map/convert_element_type | solution.py:534
  119.4 0.0 copy-done.2
  119.4 0.6 fusion
  120.0 0.1 copy-done
  120.1 1.7 %copy.17 = bf16[96,16,1024]{2,1,0:T(8,128)(2,1)} copy(bf16[96,16,1024]{2,1,0:T(8,128)(2,1)S(1)} %copy-done) | data formatting | bytes 6291456
  121.7 0.6 copy.18
Async XLA Ops:
  112.7 4.2 %copy-start.1 = (bf16[1024,1024]{1,0:T(8,128)(2,1)S(1)}, bf16[1024,1024]{1,0:T(8,128)(2,1)}, u32[]{:S(2)}) copy-start(bf16[1024,1024]{1,0:T(8,128)(2,1)} %get-tuple-element.12) | copy-start | bytes 6291460
  116.9 2.5 %copy-start.2 = (f32[16,1024]{1,0:T(8,128)S(1)}, f32[16,1024]{1,0:T(8,128)}, u32[]{:S(2)}) copy-start(f32[16,1024]{1,0:T(8,128)} %get-tuple-element.13) | copy-start | bytes 196612
  116.9 3.2 %copy-start = (bf16[96,16,1024]{2,1,0:T(8,128)(2,1)S(1)}, bf16[96,16,1024]{2,1,0:T(8,128)(2,1)}, u32[]{:S(2)}) copy-start(bf16[96,16,1024]{2,1,0:T(8,128)(2,1)} %get-tuple-element.22) | copy-start | bytes 9437188
